TPU v7x, 512 devices: a whole 4x4x16 slice. The times are simulated.
512 devices in a mesh: view: 32 (over y_hi, z), tok: 16 (over x, y_lo, core).
Axes of the slice: x: 4, y: 4 (y_hi: 2, y_lo: 2; y = y_hi * 2 + y_lo), z: 16, core: 2. Of those that a mesh axis runs over, the one named last changes fastest.
Arguments:
- queries: bfloat16 [32, 2, 2048, 1024], P('view', None, 'tok'), may hold values from -6 to 6
- keys: bfloat16 [32, 2, 2048, 1024], P('view', None, 'tok'), may hold values from -6 to 6
- values: bfloat16 [32, 2, 2048, 1024], P('view', None, 'tok'), may hold values from -6 to 6
- tile_mask: int32 [32, 2, 16, 16], P('view'), may hold values from 0 to 1, as said below
- offsets: int32 [32, 2], P('view'), may hold values from -2 to 2, as said below
- branch_slots: int32 [32, 2], replicated, may hold values from 0 to 1, each once within a row
Outputs:
- attended: bfloat16 [32, 2, 2048, 1024], P('view', None, 'tok')
Inputs may be any that keep to these rules, and one draw needn't show every extreme that they name: Each row tile_mask[v, j, t, :] holds 1 to 6 ones at consecutive tiles modulo 16; for every v and j some row holds exactly 6. `offsets`: each row holds two different values of -2, -1, 1, 2. `branch_slots`: each row is 0, 1 or 1, 0.
All inputs are finite; a program needn't handle non-finite values.
Results may differ from a plain program's by a relative error of at most 0.0049.
Values may be sent and summed in bfloat16 or wider, within the bound.
A program may use at most 64 MiB of HBM per device.

v0:
```python
import math

import jax
import jax.numpy as jnp
from jax import lax
from jax.sharding import PartitionSpec as P

HD = 64
TILE = 128
BAND = 6
NB = 2


NEG_SCORE = -1e30


def from_behind(shard, axis, by):
    size = lax.axis_size(axis)
    return lax.ppermute(shard, axis, [(i, (i + by) % size) for i in range(size)])


def fetch_views(stacked):
    nearby = {}
    for distance in (1, -1, 2, -2):
        nearby[distance] = from_behind(stacked, "view", -distance)
    return nearby


def pick_neighbour(nearby, offsets, branch_slots, member):
    offset_value = offsets[0, member]
    picked = nearby[1]
    for distance in (-1, 2, -2):
        picked = jnp.where(offset_value == distance, nearby[distance], picked)
    view_count = branch_slots.shape[0]
    view_index = lax.axis_index("view")
    other_view = (view_index + offset_value) % view_count
    rows = jnp.arange(view_count, dtype=jnp.int32)
    other_slot = jnp.sum(jnp.where(rows == other_view, branch_slots[:, 0], 0))
    own_slot = jnp.sum(jnp.where(rows == view_index, branch_slots[:, 0], 0))
    return jnp.where(other_slot != own_slot, picked[:, ::-1], picked)


def local(queries, keys, values, tile_mask, offsets, branch_slots):
    stacked = jnp.concatenate([keys, values], axis=0)
    heads_q, heads_kv = (
        lax.all_to_all(queries, "tok", split_axis=3, concat_axis=2, tiled=True),
        lax.all_to_all(stacked, "tok", split_axis=3, concat_axis=2, tiled=True),
    )
    nearby = fetch_views(heads_kv)
    first_nb = pick_neighbour(nearby, offsets, branch_slots, 0)
    second_nb = pick_neighbour(nearby, offsets, branch_slots, 1)
    tile_len = TILE
    view_len = heads_q.shape[2]
    heads_width = heads_q.shape[3]
    heads_here = heads_width // HD
    key_tiles = view_len // tile_len
    tile_most = min(BAND, key_tiles)
    group_len = math.gcd(key_tiles, max(1, 512 // tile_len))
    group_count = key_tiles // group_len
    masks = tile_mask[0]
    tile_count = jnp.sum(masks, axis=-1)
    chosen = jnp.argsort(1 - masks, axis=-1, stable=True)[..., :tile_most]
    valid = jnp.arange(tile_most, dtype=jnp.int32)[None, None, :] < tile_count[..., None]
    query_all = heads_q[0].reshape(2, key_tiles, tile_len, heads_here, HD)
    own_kv = heads_kv.reshape(2, 2, key_tiles, tile_len, heads_here, HD)
    neighbours = jnp.stack([first_nb, second_nb]).reshape(
        NB, 2, 2, key_tiles, tile_len, heads_here, HD
    )

    def block_attend(group_index):
        start = group_index * group_len
        query_block = lax.dynamic_slice_in_dim(query_all, start, group_len, 1)
        own_block = lax.dynamic_slice_in_dim(own_kv, start, group_len, 2)
        picked_tiles = lax.dynamic_slice_in_dim(chosen, start, group_len, 1)
        picked_valid = lax.dynamic_slice_in_dim(valid, start, group_len, 1)
        gathered = jnp.stack(
            [neighbours[member][:, :, picked_tiles[member]] for member in range(NB)], axis=3
        )
        gathered = gathered.reshape(2, 2, group_len, NB * tile_most * tile_len, heads_here, HD)
        key_block = jnp.concatenate([own_block, gathered], axis=3)
        keep_far = jnp.repeat(picked_valid, tile_len, axis=-1)
        keep_far = jnp.transpose(keep_far, (1, 0, 2)).reshape(group_len, NB * tile_most * tile_len)
        keep_mask = jnp.concatenate([jnp.ones((group_len, tile_len), bool), keep_far], axis=1)
        scores = jnp.einsum(
            "bgqhd,bgkhd->bghqk", query_block, key_block[0], preferred_element_type=jnp.float32
        ) * HD ** (-0.5)
        scores = jnp.where(keep_mask[None, :, None, None, :], scores, NEG_SCORE)
        row_max = jnp.max(scores, axis=-1, keepdims=True)
        expo = jnp.exp(scores - row_max)
        row_total = jnp.sum(expo, axis=-1, keepdims=True)
        weights = (expo / row_total).astype(jnp.bfloat16)
        result = jnp.einsum(
            "bghqk,bgkhd->bgqhd", weights, key_block[1], preferred_element_type=jnp.float32
        )
        return result.astype(jnp.bfloat16)

    blocks = lax.map(block_attend, jnp.arange(group_count, dtype=jnp.int32))
    attended_heads = jnp.moveaxis(blocks, 0, 1).reshape(1, 2, view_len, heads_width)
    return lax.all_to_all(attended_heads, "tok", split_axis=2, concat_axis=3, tiled=True)


def solution(mesh):
    in_specs = (
        P("view", None, "tok", None),
        P("view", None, "tok", None),
        P("view", None, "tok", None),
        P("view", None, None, None),
        P("view", None),
        P(),
    )
    out_specs = P("view", None, "tok", None)
    return jax.shard_map(local, mesh=mesh, in_specs=in_specs, out_specs=out_specs, check_vma=False)
```

profile of v0, /device:TPU:1, one launch (start us, length us, event | category | flops | bytes accessed | tf_op | source)
XLA Modules:
  0.0 265.2 jit_solution(18225511316136099209)
XLA Ops:
  2.2 24.8 %all_to_all.51 = bf16[2,2,128,1024]{2,1,0,3:T(2,128)(2,1)S(1)} all-to-all(bf16[2,2,128,1024]{2,1,0,3:T(2,128)(2,1)S(1)} %copy.43), channel_id=1, replica_groups=mesh['view'=32,'tok'=16] {'tok'}, dimensions={3} | all-to-all | bytes 2097152 | tf_op jit(solution)/shard_map/all_to_all | solution.py:47
  28.9 2.1 collective-permute-start
  31.1 10.9 %collective-permute-start.1 = (bf16[2,2,2048,64]{2,3,1,0:T(8,128)(2,1)}, bf16[2,2,2048,64]{2,3,1,0:T(8,128)(2,1)}, u32[]{:S(2)}, u32[]{:S(2)}) collective-permute-start(bf16[2,2,2048,64]{2,3,1,0:T(8,128)(2,1)} %all_to_all.40), channel_id=1, source_target_pairs={{0,480},{16,496},{32,0},{48,16},{64,32},{80,48},{96,64},{112,80},{... | collective-permute-start | bytes 3145736 | tf_op jit(solution)/shard_map/ppermute | solution.py:19
  42.0 2.6 collective-permute-start.2
  44.6 6.3 %collective-permute-start.3 = (bf16[2,2,2048,64]{2,3,1,0:T(8,128)(2,1)}, bf16[2,2,2048,64]{2,3,1,0:T(8,128)(2,1)}, u32[]{:S(2)}, u32[]{:S(2)}) collective-permute-start(bf16[2,2,2048,64]{2,3,1,0:T(8,128)(2,1)} %all_to_all.40), channel_id=1, source_target_pairs={{0,496},{16,0},{32,16},{48,32},{64,48},{80,64},{96,80},{112,96},{1... | collective-permute-start | bytes 3145736 | tf_op jit(solution)/shard_map/ppermute | solution.py:19
  52.0 5.5 %all-to-all-start.1 = ((bf16[1,2,128,1024]{2,1,0,3:T(2,128)(2,1)}), bf16[1,2,128,1024]{2,1,0,3:T(2,128)(2,1)S(1)}, u32[]{:S(2)}, u32[]{:S(2)}) async-start(bf16[1,2,128,1024]{2,1,0,3:T(2,128)(2,1)} %copy.47), calls=%async_computation.1 | async-start | bytes 1048576 | tf_op jit(solution)/shard_map/all_to_all | solution.py:46
  67.5 6.2 %all-to-all-done.1 = bf16[1,2,128,1024]{2,1,0,3:T(2,128)(2,1)S(1)} async-done(((bf16[1,2,128,1024]{2,1,0,3:T(2,128)(2,1)}), bf16[1,2,128,1024]{2,1,0,3:T(2,128)(2,1)S(1)}, u32[]{:S(2)}, u32[]{:S(2)}) %all-to-all-start.1) | async-done | bytes 524320 | tf_op jit(solution)/shard_map/all_to_all | solution.py:46
  75.9 9.7 %collective-permute-done.1 = bf16[2,2,2048,64]{2,3,1,0:T(8,128)(2,1)} collective-permute-done((bf16[2,2,2048,64]{2,3,1,0:T(8,128)(2,1)}, bf16[2,2,2048,64]{2,3,1,0:T(8,128)(2,1)}, u32[]{:S(2)}, u32[]{:S(2)}) %collective-permute-start.1) | collective-permute-done | bytes 1048608 | tf_op jit(solution)/shard_map/ppermute | solution.py:19
  85.6 22.4 %collective-permute-done.2 = bf16[2,2,2048,64]{2,3,1,0:T(8,128)(2,1)} collective-permute-done((bf16[2,2,2048,64]{2,3,1,0:T(8,128)(2,1)}, bf16[2,2,2048,64]{2,3,1,0:T(8,128)(2,1)}, u32[]{:S(2)}, u32[]{:S(2)}) %collective-permute-start.2) | collective-permute-done | bytes 1048608 | tf_op jit(solution)/shard_map/ppermute | solution.py:19
  114.8 131.0 %while.10 = (s32[]{:T(128)}, bf16[4,2,4,128,1,64]{3,5,2,1,4,0:T(8,128)(2,1)}, s32[4]{0:T(128)S(1)}, bf16[2,2,16,128,1,64]{3,5,2,1,4,0:T(8,128)(2,1)}, bf16[2,2,2...) while((s32[]{:T(128)}, ...), condition=%wide.region_8.9_spmd, body=%wide.region_5.8_spmd.sunk | while | flops 454889216 | bytes 56941580 | solution.py:97
  122.1 4.3 %copy_bitcast_fusion.6 = (bf16[2,2,4,1,6,128,1,64]{5,4,3,7,2,1,0,6:T(8,128)(2,1)S(1)}, bf16[2,2,4,1,6,128,1,64]{5,4,3,7,2,1,0,6:T(8,128)(2,1)S(1)}) fusion(bf16[4,6,2,2,128,64]{4,5,3,2,1,0:T(8,128)(2,1)S(1)} %bitcast.145, bf16[4,6,2,2,128,64]{4,5,3,2,1,0:T(8,128)(2,1)} %bitcast.146), kind=kLoop, calls=%fused_computation.14.clone.1 | loop fusion | bytes 6291456 | tf_op jit(solution)/shard_map/while/body/eval_jaxpr/stack | solution.py:76
  126.4 2.9 %pad_maximum_fusion.5 = bf16[2,2,4,2,6,128,1,64]{5,4,3,7,2,1,0,6:T(8,128)(2,1)} fusion(bf16[2,2,4,1,6,128,1,64]{5,4,3,7,2,1,0,6:T(8,128)(2,1)S(1)} %get-tuple-element.168, bf16[2,2,4,1,6,128,1,64]{5,4,3,7,2,1,0,6:T(8,128)(2,1)S(1)} %get-tuple-element.169), kind=kLoop, calls=%fused_computation.7.clone.1 | loop fusion | flops 1572864 | bytes 6291456 | tf_op jit(solution)/shard_map/while/body/eval_jaxpr/stack | solution.py:76
  129.3 6.3 %reshape.163 = bf16[2,2,4,1536,1,64]{3,5,2,1,0,4:T(8,128)(2,1)S(1)} reshape(bf16[2,2,4,2,6,128,1,64]{5,4,3,7,2,1,0,6:T(8,128)(2,1)} %pad_maximum_fusion.5) | data formatting | bytes 6291456 | tf_op jit(solution)/shard_map/while/body/eval_jaxpr/reshape | solution.py:79
  136.7 5.8 %fusion.62 = (f32[2,4,128]{2,1,0:T(4,128)S(1)}, f32[2,4,128,1664]{3,2,1,0:T(8,128)}) fusion(pred[4,1664]{1,0:T(4,128)(4,1)S(1)} %concatenate.12, bf16[2,2,4,1536,1,64]{3,5,2,1,4,0:T(8,128)(2,1)S(1)} %bitcast.147, bf16[2,2,4,128,1,64]{3,5,2,1,4,0:T(8,128)(2,1)S(1)} %constant_dynamic-slice_fusion.5, ...), kind=kOutput, calls=%fused_computation.63.clone.1 | convolution fusion | flops 228329088 | bytes 10365444 | tf_op jit(solution)/shard_map/while/body/eval_jaxpr/sub | solution.py:89
  142.5 5.0 %fusion.63 = bf16[4,2,4,128,1,64]{3,5,2,1,4,0:T(8,128)(2,1)} fusion(bf16[4,2,4,128,1,64]{3,5,2,1,4,0:T(8,128)(2,1)} %get-tuple-element.187, s32[]{:T(128)} %get-tuple-element.186, f32[2,4,128,1664]{3,2,1,0:T(8,128)} %get-tuple-element.170, f32[2,4,128]{2,1,0:T(4,128)S(1)} %get-tuple-element.171, ...), kind=kOutput, calls=%fused_computation.24.clone.1 | convolution fusion | flops 224985088 | bytes 10359296 | tf_op jit(solution)/shard_map/while/body/eval_jaxpr/bghqk,bgkhd->bgqhd/dot_general | solution.py:92
  154.8 4.3 %copy_bitcast_fusion.6 = (bf16[2,2,4,1,6,128,1,64]{5,4,3,7,2,1,0,6:T(8,128)(2,1)S(1)}, bf16[2,2,4,1,6,128,1,64]{5,4,3,7,2,1,0,6:T(8,128)(2,1)S(1)}) fusion(bf16[4,6,2,2,128,64]{4,5,3,2,1,0:T(8,128)(2,1)S(1)} %bitcast.145, bf16[4,6,2,2,128,64]{4,5,3,2,1,0:T(8,128)(2,1)} %bitcast.146), kind=kLoop, calls=%fused_computation.14.clone.1 | loop fusion | bytes 6291456 | tf_op jit(solution)/shard_map/while/body/eval_jaxpr/stack | solution.py:76
  159.1 2.9 %pad_maximum_fusion.5 = bf16[2,2,4,2,6,128,1,64]{5,4,3,7,2,1,0,6:T(8,128)(2,1)} fusion(bf16[2,2,4,1,6,128,1,64]{5,4,3,7,2,1,0,6:T(8,128)(2,1)S(1)} %get-tuple-element.168, bf16[2,2,4,1,6,128,1,64]{5,4,3,7,2,1,0,6:T(8,128)(2,1)S(1)} %get-tuple-element.169), kind=kLoop, calls=%fused_computation.7.clone.1 | loop fusion | flops 1572864 | bytes 6291456 | tf_op jit(solution)/shard_map/while/body/eval_jaxpr/stack | solution.py:76
  162.0 6.3 %reshape.163 = bf16[2,2,4,1536,1,64]{3,5,2,1,0,4:T(8,128)(2,1)S(1)} reshape(bf16[2,2,4,2,6,128,1,64]{5,4,3,7,2,1,0,6:T(8,128)(2,1)} %pad_maximum_fusion.5) | data formatting | bytes 6291456 | tf_op jit(solution)/shard_map/while/body/eval_jaxpr/reshape | solution.py:79
  169.4 5.8 %fusion.62 = (f32[2,4,128]{2,1,0:T(4,128)S(1)}, f32[2,4,128,1664]{3,2,1,0:T(8,128)}) fusion(pred[4,1664]{1,0:T(4,128)(4,1)S(1)} %concatenate.12, bf16[2,2,4,1536,1,64]{3,5,2,1,4,0:T(8,128)(2,1)S(1)} %bitcast.147, bf16[2,2,4,128,1,64]{3,5,2,1,4,0:T(8,128)(2,1)S(1)} %constant_dynamic-slice_fusion.5, ...), kind=kOutput, calls=%fused_computation.63.clone.1 | convolution fusion | flops 228329088 | bytes 10365444 | tf_op jit(solution)/shard_map/while/body/eval_jaxpr/sub | solution.py:89
  175.3 5.0 %fusion.63 = bf16[4,2,4,128,1,64]{3,5,2,1,4,0:T(8,128)(2,1)} fusion(bf16[4,2,4,128,1,64]{3,5,2,1,4,0:T(8,128)(2,1)} %get-tuple-element.187, s32[]{:T(128)} %get-tuple-element.186, f32[2,4,128,1664]{3,2,1,0:T(8,128)} %get-tuple-element.170, f32[2,4,128]{2,1,0:T(4,128)S(1)} %get-tuple-element.171, ...), kind=kOutput, calls=%fused_computation.24.clone.1 | convolution fusion | flops 224985088 | bytes 10359296 | tf_op jit(solution)/shard_map/while/body/eval_jaxpr/bghqk,bgkhd->bgqhd/dot_general | solution.py:92
  187.6 4.3 %copy_bitcast_fusion.6 = (bf16[2,2,4,1,6,128,1,64]{5,4,3,7,2,1,0,6:T(8,128)(2,1)S(1)}, bf16[2,2,4,1,6,128,1,64]{5,4,3,7,2,1,0,6:T(8,128)(2,1)S(1)}) fusion(bf16[4,6,2,2,128,64]{4,5,3,2,1,0:T(8,128)(2,1)S(1)} %bitcast.145, bf16[4,6,2,2,128,64]{4,5,3,2,1,0:T(8,128)(2,1)} %bitcast.146), kind=kLoop, calls=%fused_computation.14.clone.1 | loop fusion | bytes 6291456 | tf_op jit(solution)/shard_map/while/body/eval_jaxpr/stack | solution.py:76
  191.9 2.9 %pad_maximum_fusion.5 = bf16[2,2,4,2,6,128,1,64]{5,4,3,7,2,1,0,6:T(8,128)(2,1)} fusion(bf16[2,2,4,1,6,128,1,64]{5,4,3,7,2,1,0,6:T(8,128)(2,1)S(1)} %get-tuple-element.168, bf16[2,2,4,1,6,128,1,64]{5,4,3,7,2,1,0,6:T(8,128)(2,1)S(1)} %get-tuple-element.169), kind=kLoop, calls=%fused_computation.7.clone.1 | loop fusion | flops 1572864 | bytes 6291456 | tf_op jit(solution)/shard_map/while/body/eval_jaxpr/stack | solution.py:76
  194.8 6.3 %reshape.163 = bf16[2,2,4,1536,1,64]{3,5,2,1,0,4:T(8,128)(2,1)S(1)} reshape(bf16[2,2,4,2,6,128,1,64]{5,4,3,7,2,1,0,6:T(8,128)(2,1)} %pad_maximum_fusion.5) | data formatting | bytes 6291456 | tf_op jit(solution)/shard_map/while/body/eval_jaxpr/reshape | solution.py:79
  202.2 5.8 %fusion.62 = (f32[2,4,128]{2,1,0:T(4,128)S(1)}, f32[2,4,128,1664]{3,2,1,0:T(8,128)}) fusion(pred[4,1664]{1,0:T(4,128)(4,1)S(1)} %concatenate.12, bf16[2,2,4,1536,1,64]{3,5,2,1,4,0:T(8,128)(2,1)S(1)} %bitcast.147, bf16[2,2,4,128,1,64]{3,5,2,1,4,0:T(8,128)(2,1)S(1)} %constant_dynamic-slice_fusion.5, ...), kind=kOutput, calls=%fused_computation.63.clone.1 | convolution fusion | flops 228329088 | bytes 10365444 | tf_op jit(solution)/shard_map/while/body/eval_jaxpr/sub | solution.py:89
  208.0 5.0 %fusion.63 = bf16[4,2,4,128,1,64]{3,5,2,1,4,0:T(8,128)(2,1)} fusion(bf16[4,2,4,128,1,64]{3,5,2,1,4,0:T(8,128)(2,1)} %get-tuple-element.187, s32[]{:T(128)} %get-tuple-element.186, f32[2,4,128,1664]{3,2,1,0:T(8,128)} %get-tuple-element.170, f32[2,4,128]{2,1,0:T(4,128)S(1)} %get-tuple-element.171, ...), kind=kOutput, calls=%fused_computation.24.clone.1 | convolution fusion | flops 224985088 | bytes 10359296 | tf_op jit(solution)/shard_map/while/body/eval_jaxpr/bghqk,bgkhd->bgqhd/dot_general | solution.py:92
  220.3 4.3 %copy_bitcast_fusion.6 = (bf16[2,2,4,1,6,128,1,64]{5,4,3,7,2,1,0,6:T(8,128)(2,1)S(1)}, bf16[2,2,4,1,6,128,1,64]{5,4,3,7,2,1,0,6:T(8,128)(2,1)S(1)}) fusion(bf16[4,6,2,2,128,64]{4,5,3,2,1,0:T(8,128)(2,1)S(1)} %bitcast.145, bf16[4,6,2,2,128,64]{4,5,3,2,1,0:T(8,128)(2,1)} %bitcast.146), kind=kLoop, calls=%fused_computation.14.clone.1 | loop fusion | bytes 6291456 | tf_op jit(solution)/shard_map/while/body/eval_jaxpr/stack | solution.py:76
  224.7 2.9 %pad_maximum_fusion.5 = bf16[2,2,4,2,6,128,1,64]{5,4,3,7,2,1,0,6:T(8,128)(2,1)} fusion(bf16[2,2,4,1,6,128,1,64]{5,4,3,7,2,1,0,6:T(8,128)(2,1)S(1)} %get-tuple-element.168, bf16[2,2,4,1,6,128,1,64]{5,4,3,7,2,1,0,6:T(8,128)(2,1)S(1)} %get-tuple-element.169), kind=kLoop, calls=%fused_computation.7.clone.1 | loop fusion | flops 1572864 | bytes 6291456 | tf_op jit(solution)/shard_map/while/body/eval_jaxpr/stack | solution.py:76
  227.5 6.3 %reshape.163 = bf16[2,2,4,1536,1,64]{3,5,2,1,0,4:T(8,128)(2,1)S(1)} reshape(bf16[2,2,4,2,6,128,1,64]{5,4,3,7,2,1,0,6:T(8,128)(2,1)} %pad_maximum_fusion.5) | data formatting | bytes 6291456 | tf_op jit(solution)/shard_map/while/body/eval_jaxpr/reshape | solution.py:79
  234.9 5.8 %fusion.62 = (f32[2,4,128]{2,1,0:T(4,128)S(1)}, f32[2,4,128,1664]{3,2,1,0:T(8,128)}) fusion(pred[4,1664]{1,0:T(4,128)(4,1)S(1)} %concatenate.12, bf16[2,2,4,1536,1,64]{3,5,2,1,4,0:T(8,128)(2,1)S(1)} %bitcast.147, bf16[2,2,4,128,1,64]{3,5,2,1,4,0:T(8,128)(2,1)S(1)} %constant_dynamic-slice_fusion.5, ...), kind=kOutput, calls=%fused_computation.63.clone.1 | convolution fusion | flops 228329088 | bytes 10365444 | tf_op jit(solution)/shard_map/while/body/eval_jaxpr/sub | solution.py:89
  240.8 5.0 %fusion.63 = bf16[4,2,4,128,1,64]{3,5,2,1,4,0:T(8,128)(2,1)} fusion(bf16[4,2,4,128,1,64]{3,5,2,1,4,0:T(8,128)(2,1)} %get-tuple-element.187, s32[]{:T(128)} %get-tuple-element.186, f32[2,4,128,1664]{3,2,1,0:T(8,128)} %get-tuple-element.170, f32[2,4,128]{2,1,0:T(4,128)S(1)} %get-tuple-element.171, ...), kind=kOutput, calls=%fused_computation.24.clone.1 | convolution fusion | flops 224985088 | bytes 10359296 | tf_op jit(solution)/shard_map/while/body/eval_jaxpr/bghqk,bgkhd->bgqhd/dot_general | solution.py:92
  245.8 2.4 copy.57
  248.9 13.9 %all_to_all.52 = bf16[16,2,8192]{2,1,0:T(2,128)(2,1)S(1)} all-to-all(bf16[16,2,8192]{2,1,0:T(2,128)(2,1)S(1)} %reshape.146), channel_id=1, replica_groups=mesh['view'=32,'tok'=16] {'tok'}, dimensions={0} | all-to-all | bytes 1048576 | tf_op jit(solution)/shard_map/all_to_all | solution.py:99
  (103 shorter events, 50.6 us)
Async XLA Ops:
  2.2 48.7 %copy-start.1 = (bf16[1,2,128,1024]{3,2,1,0:T(8,128)(2,1)S(1)}, bf16[1,2,128,1024]{3,2,1,0:T(8,128)(2,1)}, u32[]{:S(2)}) copy-start(bf16[1,2,128,1024]{3,2,1,0:T(8,128)(2,1)} %param.8) | copy-start | bytes 1572868
  26.9 30.6 %copy-start.3 = (s32[1,2]{1,0:T(1,128)S(1)}, s32[1,2]{1,0:T(1,128)}, u32[]{:S(2)}) copy-start(s32[1,2]{1,0:T(1,128)} %param.12) | copy-start | bytes 28
  26.9 32.4 %copy-start.4 = (s32[32,2]{0,1:T(2,128)S(1)}, s32[32,2]{0,1:T(2,128)}, u32[]{:S(2)}) copy-start(s32[32,2]{0,1:T(2,128)} %param.13) | copy-start | bytes 772
  26.9 36.8 %copy-start.2 = (s32[1,2,16,16]{3,2,1,0:T(8,128)S(1)}, s32[1,2,16,16]{3,2,1,0:T(8,128)}, u32[]{:S(2)}) copy-start(s32[1,2,16,16]{3,2,1,0:T(8,128)} %param.11) | copy-start | bytes 6148
  28.9 47.0 %collective-permute-start = (bf16[2,2,2048,64]{2,3,1,0:T(8,128)(2,1)}, bf16[2,2,2048,64]{2,3,1,0:T(8,128)(2,1)S(1)}, u32[]{:S(2)}, u32[]{:S(2)}) collective-permute-start(bf16[2,2,2048,64]{2,3,1,0:T(8,128)(2,1)} %all_to_all.40), channel_id=1, source_target_pairs={{0,32},{16,48},{32,64},{48,80},{64,96},{80,112},{96,128},{112,144}... | collective-permute-start | bytes 3145736 | tf_op jit(solution)/shard_map/ppermute | solution.py:19
  31.1 54.5 %collective-permute-start.1 = (bf16[2,2,2048,64]{2,3,1,0:T(8,128)(2,1)}, bf16[2,2,2048,64]{2,3,1,0:T(8,128)(2,1)}, u32[]{:S(2)}, u32[]{:S(2)}) collective-permute-start(bf16[2,2,2048,64]{2,3,1,0:T(8,128)(2,1)} %all_to_all.40), channel_id=1, source_target_pairs={{0,480},{16,496},{32,0},{48,16},{64,32},{80,48},{96,64},{112,80},{... | collective-permute-start | bytes 3145736 | tf_op jit(solution)/shard_map/ppermute | solution.py:19
  42.0 66.0 %collective-permute-start.2 = (bf16[2,2,2048,64]{2,3,1,0:T(8,128)(2,1)}, bf16[2,2,2048,64]{2,3,1,0:T(8,128)(2,1)}, u32[]{:S(2)}, u32[]{:S(2)}) collective-permute-start(bf16[2,2,2048,64]{2,3,1,0:T(8,128)(2,1)} %all_to_all.40), channel_id=1, source_target_pairs={{0,16},{16,32},{32,48},{48,64},{64,80},{80,96},{96,112},{112,128},... | collective-permute-start | bytes 3145736 | tf_op jit(solution)/shard_map/ppermute | solution.py:19
  44.6 64.9 %collective-permute-start.3 = (bf16[2,2,2048,64]{2,3,1,0:T(8,128)(2,1)}, bf16[2,2,2048,64]{2,3,1,0:T(8,128)(2,1)}, u32[]{:S(2)}, u32[]{:S(2)}) collective-permute-start(bf16[2,2,2048,64]{2,3,1,0:T(8,128)(2,1)} %all_to_all.40), channel_id=1, source_target_pairs={{0,496},{16,0},{32,16},{48,32},{64,48},{80,64},{96,80},{112,96},{1... | collective-permute-start | bytes 3145736 | tf_op jit(solution)/shard_map/ppermute | solution.py:19
  52.0 21.6 %all-to-all-start.1 = ((bf16[1,2,128,1024]{2,1,0,3:T(2,128)(2,1)}), bf16[1,2,128,1024]{2,1,0,3:T(2,128)(2,1)S(1)}, u32[]{:S(2)}, u32[]{:S(2)}) async-start(bf16[1,2,128,1024]{2,1,0,3:T(2,128)(2,1)} %copy.47), calls=%async_computation.1 | async-start | bytes 1048576 | tf_op jit(solution)/shard_map/all_to_all | solution.py:46
  120.1 2.0 copy-start
  152.9 2.0 copy-start
  185.6 2.0 copy-start
  218.4 2.0 copy-start
where the time goes:
time: 267 us; the launch traced here: 265 us
  local copies, waits for them, and re-layouts  87.7 us (33%)
  matrix products  43.5 us (16%)
  waiting for transfers between devices  39.9 us (15%)
  blocking collectives  38.7 us (14%)
  starting transfers between devices  27.5 us (10%)
  other arithmetic  17.4 us (7%)
  between operations  7.59 us (3%)
  loops' own time  2.99 us (1%)
    ppermute x4, waiting for transfers between devices, from_behind(): lax.ppermute(shard, axis, [(i, (i + by) % size) for i in range(size)])  33.7 us
    reshape x4, local copies, waits for them, and re-layouts, block_attend(): gathered.reshape(2, 2, group_len, NB * tile_most * tile_len, heads_here, HD)  25 us
    all_to_all x1, blocking collectives, local(): lax.all_to_all(stacked, 'tok', split_axis=3, concat_axis=2, tiled=True)  24.8 us
    sub x4, matrix products, block_attend(): expo = jnp.exp(scores - row_max)  23.4 us
    ppermute x4, starting transfers between devices, from_behind(): lax.ppermute(shard, axis, [(i, (i + by) % size) for i in range(size)])  22 us
    dot_general x4, matrix products, block_attend(): jnp.einsum('bghqk,bgkhd->bgqhd', weights, key_block[1], preferred_element...  20.1 us
    another operation x4, local copies, waits for them, and re-layouts, block_attend(): jnp.stack([neighbours[member][:, :, picked_tiles[member]] for member in r...  17.3 us
    gather x8, local copies, waits for them, and re-layouts, block_attend(): neighbours[member][:, :, picked_tiles[member]]  15.6 us
  transfers between devices with their start and end apart: 5, of which 4 were waited for; matrix products, arithmetic and copies ran while one was open for 2% of the time, Pallas kernels for 0%

commit v1 on v0

v1 whole, which is shorter than its diff:
```python
import jax
import jax.numpy as jnp
from jax import lax
from jax.experimental import pallas as pl
from jax.experimental.pallas import tpu as pltpu
from jax.sharding import PartitionSpec as P

MESH = pl.DeviceIdType.MESH
TILE = 128
LANES = 128
HD = 64
BAND = 6
NB = 2
KEY_COLS = 1 + NB * BAND
NEG_SCORE = -1e30
XS = 4
ROWS = 64
GX = (0, 1, 3, 2)


def attend_kernel(
    mask_ref, off_ref, slot_ref, q_ref, k_ref, v_ref, out_ref,
    raw_k, raw_v, raw_q, stage, qbuf, kbuf, vbuf, sbuf, wbuf, obuf, orecv, ost, start_s, count_s,
    in_sem, a_send, a_recv, z_send, z_recv, o_send, o_recv, out_sem,
):
    views = lax.axis_size("view")
    toks = lax.axis_size("tok")
    group = toks // XS
    view = lax.axis_index("view")
    me = lax.axis_index("tok")
    right = lax.rem(view + 1, views)
    left = lax.rem(view + views - 1, views)
    my_x = me // group
    my_r = lax.rem(me, group)
    bufs = (kbuf, vbuf, qbuf)
    raws = (raw_k, raw_v, raw_q)

    def remote(src, dst, send, recv, dev):
        return pltpu.make_async_remote_copy(
            src_ref=src, dst_ref=dst, send_sem=send, recv_sem=recv, device_id=dev, device_id_type=MESH
        )

    def in_copy(a):
        return pltpu.make_async_copy((k_ref, v_ref, q_ref)[a].at[0], raws[a], in_sem.at[a])

    for a in range(3):
        in_copy(a).start()

    barrier = pltpu.get_barrier_semaphore()
    for d in range(1, 16):
        pl.semaphore_signal(barrier, inc=1, device_id=(view, lax.rem(me + d, toks)), device_id_type=MESH)
    for to in (right, left):
        pl.semaphore_signal(barrier, inc=1, device_id=(to, me), device_id_type=MESH)

    first_slot = slot_ref[view, 0]

    def stage_array(a):
        in_copy(a).wait()
        for b in range(2):
            slot = first_slot if b == 0 else 1 - first_slot
            for p in range(8):
                stage[a, p * 2 + b] = raws[a][slot, :, p * LANES:(p + 1) * LANES]
        bufs[a][me] = stage[a, me]

    def a2a_copy(a, dest):
        return remote(stage.at[a, dest], bufs[a].at[me], a_send.at[a, dest], a_recv.at[a, me], (view, dest))

    def a2a_send(a):
        for gx in GX:
            for r in range(4):
                if (gx, r) != (0, 0):
                    dest = lax.rem(my_x + gx, XS) * group + lax.rem(my_r + r, group)
                    a2a_copy(a, dest).start()

    def a2a_wait(a, gx):
        for r in range(4):
            if (gx, r) != (0, 0):
                src = lax.rem(my_x + XS - gx, XS) * group + lax.rem(my_r + group - r, group)
                remote(stage.at[a, 0], bufs[a].at[src], a_send.at[a, 0], a_recv.at[a, src], (view, src)).wait_recv()

    def z_copy(a, hop, gi, gx):
        start = lax.rem(my_x + XS - gx, XS) * group
        src_set, dst_set, dev = ((0, 1, right), (0, 2, left), (1, 3, right), (2, 4, left))[hop]
        return remote(
            bufs[a].at[pl.ds(src_set * toks + start, 4)],
            bufs[a].at[pl.ds(dst_set * toks + start, 4)],
            z_send.at[a, hop, gi], z_recv.at[a, hop, gi], (dev, me),
        )

    stage_array(0)
    pl.semaphore_wait(barrier, 17)
    a2a_send(0)
    a2a_wait(0, GX[0])
    for hop in (0, 1):
        z_copy(0, hop, 0, GX[0]).start()
    stage_array(1)
    a2a_send(1)
    a2a_wait(0, GX[1])
    for hop in (0, 1):
        z_copy(0, hop, 1, GX[1]).start()
    stage_array(2)
    a2a_send(2)
    for gi in (2, 3):
        a2a_wait(0, GX[gi])
        for hop in (0, 1):
            z_copy(0, hop, gi, GX[gi]).start()
    for gi in range(4):
        for hop in (0, 1):
            z_copy(0, hop, gi, GX[gi]).wait_recv()
            z_copy(0, hop + 2, gi, GX[gi]).start()
    for gi in range(4):
        a2a_wait(1, GX[gi])
        for hop in (0, 1):
            z_copy(1, hop, gi, GX[gi]).start()

    for j in range(NB):
        def count_row(t, carry, j=j):
            first = jnp.int32(0)
            total = jnp.int32(0)
            before = mask_ref[0, j, t, 15]
            for k in range(16):
                here = mask_ref[0, j, t, k]
                total = total + here
                first = first + jnp.where((here == 1) & (before == 0), k, 0)
                before = here
            start_s[j, t] = first
            count_s[j, t] = total
            return carry
        lax.fori_loop(0, 16, count_row, 0)

    for gx in GX:
        a2a_wait(2, gx)
    for gi in range(4):
        for hop in (2, 3):
            z_copy(0, hop, gi, GX[gi]).wait_recv()

    sets = []
    for j in range(NB):
        off = off_ref[0, j]
        sets.append(jnp.where(off == -1, 1, jnp.where(off == 1, 2, jnp.where(off == -2, 3, 4))) * toks)
    low = lax.broadcasted_iota(jnp.int32, (TILE, LANES), 1) < HD

    def tile_at(j, t, i):
        return sets[j] + lax.rem(start_s[j, t] + i, 16)

    def dot_t(x, y):
        return lax.dot_general(x, y, (((1,), (1,)), ((), ())), preferred_element_type=jnp.float32)

    def weigh_tile(t):
        q = qbuf[t] * jnp.bfloat16(0.125)
        zero = jnp.zeros_like(q)
        both = jnp.concatenate([jnp.where(low, q, zero), jnp.where(low, zero, q)], axis=0)
        sbuf[:, :LANES] = dot_t(both, kbuf[t])
        for j in range(NB):
            for i in range(0, BAND, 2):
                keys = jnp.concatenate([kbuf[tile_at(j, t, i)], kbuf[tile_at(j, t, i + 1)]], axis=0)
                s = dot_t(both, keys)
                for h in range(2):
                    bias = jnp.where(i + h < count_s[j, t], jnp.float32(0), jnp.float32(NEG_SCORE))
                    c = 1 + j * BAND + i + h
                    sbuf[:, c * LANES:(c + 1) * LANES] = s[:, h * LANES:(h + 1) * LANES] + bias
        for rb in range(0, 2 * TILE, ROWS):
            rows = pl.ds(rb, ROWS)
            top = sbuf[rows, :LANES]
            for c in range(1, KEY_COLS):
                top = jnp.maximum(top, sbuf[rows, c * LANES:(c + 1) * LANES])
            top = jnp.max(top, axis=1, keepdims=True)
            total = jnp.zeros((ROWS, LANES), jnp.float32)
            for c in range(KEY_COLS):
                e = jnp.exp(sbuf[rows, c * LANES:(c + 1) * LANES] - top)
                sbuf[rows, c * LANES:(c + 1) * LANES] = e
                total = total + e
            inv = 1.0 / jnp.sum(total, axis=1, keepdims=True)
            for c in range(KEY_COLS):
                wbuf[t, rows, c * LANES:(c + 1) * LANES] = (
                    sbuf[rows, c * LANES:(c + 1) * LANES] * inv
                ).astype(jnp.bfloat16)

    def weigh_group(gi, carry):
        lax.fori_loop(0, 4, lambda i, c: (weigh_tile(gi * 4 + i), c)[1], 0)
        gx = gi + (gi // 2) * (1 - 2 * lax.rem(gi, 2))
        for hop in (0, 1):
            z_copy(1, hop, gi, gx).wait_recv()
            z_copy(1, hop + 2, gi, gx).start()
        return carry

    lax.fori_loop(0, 4, weigh_group, 0)
    for gi in range(4):
        for hop in (2, 3):
            z_copy(1, hop, gi, GX[gi]).wait_recv()

    def o_copy(t):
        return remote(obuf.at[t], orecv.at[me], o_send.at[t], o_recv.at[me], (view, t))

    def sum_tile(d, carry):
        t = lax.rem(me + 1 + d, toks)
        parts = [vbuf[t]]
        for j in range(NB):
            parts += [vbuf[tile_at(j, t, i)] for i in range(BAND)]
        acc = jnp.dot(wbuf[t], jnp.concatenate(parts, axis=0), preferred_element_type=jnp.float32)
        obuf[t] = jnp.where(low, acc[:TILE], acc[TILE:]).astype(jnp.bfloat16)

        @pl.when(t != me)
        def _():
            o_copy(t).start()

        return carry

    lax.fori_loop(0, 16, sum_tile, 0)
    orecv[me] = obuf[me]

    for d in range(1, 16):
        src = lax.rem(me + toks - d, toks)
        remote(obuf.at[0], orecv.at[src], o_send.at[0], o_recv.at[src], (view, src)).wait_recv()
    for s in range(2):
        role = first_slot if s == 0 else 1 - first_slot
        for p in range(8):
            ost[s, :, p * LANES:(p + 1) * LANES] = orecv[p * 2 + role]
    pltpu.make_async_copy(ost, out_ref.at[0], out_sem).start()

    for d in range(1, 16):
        peer = lax.rem(me + d, toks)
        for a in range(3):
            a2a_copy(a, peer).wait_send()
        o_copy(peer).wait_send()
    for a in range(2):
        for hop in range(4):
            for gi in range(4):
                z_copy(a, hop, gi, GX[gi]).wait_send()
    pltpu.make_async_copy(ost, out_ref.at[0], out_sem).wait()


def local(queries, keys, values, tile_mask, offsets, branch_slots):
    bf16 = jnp.bfloat16
    smem = pl.BlockSpec(memory_space=pltpu.SMEM)
    hbm = pl.BlockSpec(memory_space=pl.ANY)
    dma = pltpu.SemaphoreType.DMA
    return pl.pallas_call(
        attend_kernel,
        out_shape=jax.ShapeDtypeStruct(queries.shape, bf16),
        in_specs=[smem, smem, smem, hbm, hbm, hbm],
        out_specs=hbm,
        scratch_shapes=[
            pltpu.VMEM((2, TILE, 1024), bf16),
            pltpu.VMEM((2, TILE, 1024), bf16),
            pltpu.VMEM((2, TILE, 1024), bf16),
            pltpu.VMEM((3, 16, TILE, LANES), bf16),
            pltpu.VMEM((16, TILE, LANES), bf16),
            pltpu.VMEM((80, TILE, LANES), bf16),
            pltpu.VMEM((80, TILE, LANES), bf16),
            pltpu.VMEM((2 * TILE, KEY_COLS * LANES), jnp.float32),
            pltpu.VMEM((16, 2 * TILE, KEY_COLS * LANES), bf16),
            pltpu.VMEM((16, TILE, LANES), bf16),
            pltpu.VMEM((16, TILE, LANES), bf16),
            pltpu.VMEM((2, TILE, 1024), bf16),
            pltpu.SMEM((NB, 16), jnp.int32),
            pltpu.SMEM((NB, 16), jnp.int32),
            dma((3,)),
            dma((3, 16)),
            dma((3, 16)),
            dma((2, 4, 4)),
            dma((2, 4, 4)),
            dma((16,)),
            dma((16,)),
            dma(()),
        ],
        compiler_params=pltpu.CompilerParams(
            collective_id=0, has_side_effects=True, vmem_limit_bytes=48 * 1024 * 1024
        ),
        cost_estimate=pl.CostEstimate(flops=3_500_000_000, bytes_accessed=2 << 20, transcendentals=7_000_000),
    )(tile_mask, offsets, branch_slots, queries, keys, values)


def solution(mesh):
    in_specs = (
        P("view", None, "tok", None),
        P("view", None, "tok", None),
        P("view", None, "tok", None),
        P("view", None, None, None),
        P("view", None),
        P(),
    )
    out_specs = P("view", None, "tok", None)
    return jax.shard_map(local, mesh=mesh, in_specs=in_specs, out_specs=out_specs, check_vma=False)
```

time: 267 us -> 140 us (0.52)
  Pallas kernels: 0 us -> 133 us
  local copies, waits for them, and re-layouts: 87.7 us -> 4.7 us
  matrix products: 43.5 us -> 0 us
  waiting for transfers between devices: 39.9 us -> 0 us
  blocking collectives: 38.7 us -> 0 us
  starting transfers between devices: 27.5 us -> 0 us
  other arithmetic: 17.4 us -> 0 us
  between operations: 7.59 us -> 0.02 us
  loops' own time: 2.99 us -> 0 us
    pallas_call x0 -> x1, Pallas kernels: none -> 133 us  [local(): pl.pallas_call(attend_kernel, out_shape=jax.ShapeDtypeStruct(queries.shap...]
    all_to_all x2 -> x0, blocking collectives: 38.7 us -> none  [the longest x1 24.8 us: local(): lax.all_to_all(stacked, 'tok', split_axis=3, concat_axis=2, tiled=True)]
    ppermute x4 -> x0, waiting for transfers between devices: 33.7 us -> none  [from_behind(): lax.ppermute(shard, axis, [(i, (i + by) % size) for i in range(size)])]
    reshape x9 -> x0, local copies, waits for them, and re-layouts: 27.5 us -> none  [the longest x4 25 us: block_attend(): gathered.reshape(2, 2, group_len, NB * tile_most * tile_len, heads_here, HD)]
    sub x4 -> x0, matrix products: 23.4 us -> none  [block_attend(): expo = jnp.exp(scores - row_max)]
    ppermute x4 -> x0, starting transfers between devices: 22 us -> none  [from_behind(): lax.ppermute(shard, axis, [(i, (i + by) % size) for i in range(size)])]
    dot_general x4 -> x0, matrix products: 20.1 us -> none  [block_attend(): jnp.einsum('bghqk,bgkhd->bgqhd', weights, key_block[1], preferred_element...]
    another operation x4 -> x0, local copies, waits for them, and re-layouts: 17.3 us -> none  [block_attend(): jnp.stack([neighbours[member][:, :, picked_tiles[member]] for member in r...]
  transfers between devices with their start and end apart: 5 -> 0, of which waited for: 4 -> 0; matrix products, arithmetic and copies ran while one was open for 2% -> 0% of each run, Pallas kernels for 0% -> 0%
where the time goes in v1:
time: 140 us; the launch traced here: 138 us
  Pallas kernels  133 us (95%)
  local copies, waits for them, and re-layouts  4.7 us (3%)
    pallas_call x1, Pallas kernels, local(): pl.pallas_call(attend_kernel, out_shape=jax.ShapeDtypeStruct(queries.shap...  133 us
    unnamed x12, local copies, waits for them, and re-layouts  4.7 us

profile of v1, /device:TPU:1, one launch (start us, length us, event | category | flops | bytes accessed | tf_op | source)
XLA Modules:
  0.0 137.7 jit_solution(10599735001775012674)
XLA Ops:
  0.0 0.0 copy-start.4
  0.0 0.0 copy-start.3
  0.0 0.8 copy.7.slot_ref
  0.8 0.0 copy-done.4
  0.8 0.0 copy-done.3
  0.8 0.0 copy-start
  0.8 1.0 copy-done
  1.8 0.0 copy-start.1
  1.8 1.0 copy-done.1
  2.9 0.0 copy-start.2
  2.9 1.0 copy-done.2
  3.9 133.0 %shard_map.64 = bf16[1,2,128,1024]{3,2,1,0:T(8,128)(2,1)S(1)} custom-call(s32[1,2,16,16]{3,2,1,0:T(8,128)S(1)} %copy-done.3, s32[1,2]{1,0:T(1,128)S(1)} %copy-done.4, s32[32,2]{1,0:T(8,128)S(1)} %copy.7.slot_ref, bf16[1,2,128,1024]{3,2,1,0:T(8,128)(2,1)S(1)} %copy-done, bf16[1,2,128,1024]{3,2,1,0:T(8,128)(2,1)S(1)} %copy-done.1, ...), custom_call_target="tpu_custom_call" | custom-call | flops 3500000000 | bytes 2097152 | tf_op jit(solution)/shard_map/pallas_call | solution.py:238
  137.0 0.8 copy.9
Async XLA Ops:
  0.0 0.8 copy-start.4
  0.0 0.8 copy-start.3
  0.8 1.0 copy-start
  1.8 1.0 copy-start.1
  2.9 1.0 copy-start.2

commit v2 on v1

--- a/solution.py
+++ b/solution.py
@@ -32,6 +32,17 @@
     left = lax.rem(view + views - 1, views)
     my_x = me // group
     my_r = lax.rem(me, group)
+    half = views // 2
+    upper = view // half
+
+    def flip(tok, by):
+        return tok + by * (2 - 4 * lax.rem(tok // 2, 2))
+
+    def unit_of(tok):
+        return flip(tok, upper)
+
+    right_dev = (right, flip(me, lax.rem(upper + right // half, 2)))
+    left_dev = (left, flip(me, lax.rem(upper + left // half, 2)))
     bufs = (kbuf, vbuf, qbuf)
     raws = (raw_k, raw_v, raw_q)
 
@@ -49,8 +60,8 @@
     barrier = pltpu.get_barrier_semaphore()
     for d in range(1, 16):
         pl.semaphore_signal(barrier, inc=1, device_id=(view, lax.rem(me + d, toks)), device_id_type=MESH)
-    for to in (right, left):
-        pl.semaphore_signal(barrier, inc=1, device_id=(to, me), device_id_type=MESH)
+    for to in (right_dev, left_dev):
+        pl.semaphore_signal(barrier, inc=1, device_id=to, device_id_type=MESH)
 
     first_slot = slot_ref[view, 0]
 
@@ -60,10 +71,10 @@
             slot = first_slot if b == 0 else 1 - first_slot
             for p in range(8):
                 stage[a, p * 2 + b] = raws[a][slot, :, p * LANES:(p + 1) * LANES]
-        bufs[a][me] = stage[a, me]
+        bufs[a][me] = stage[a, unit_of(me)]
 
     def a2a_copy(a, dest):
-        return remote(stage.at[a, dest], bufs[a].at[me], a_send.at[a, dest], a_recv.at[a, me], (view, dest))
+        return remote(stage.at[a, unit_of(dest)], bufs[a].at[me], a_send.at[a, dest], a_recv.at[a, me], (view, dest))
 
     def a2a_send(a):
         for gx in GX:
@@ -80,11 +91,11 @@
 
     def z_copy(a, hop, gi, gx):
         start = lax.rem(my_x + XS - gx, XS) * group
-        src_set, dst_set, dev = ((0, 1, right), (0, 2, left), (1, 3, right), (2, 4, left))[hop]
+        src_set, dst_set, dev = ((0, 1, right_dev), (0, 2, left_dev), (1, 3, right_dev), (2, 4, left_dev))[hop]
         return remote(
             bufs[a].at[pl.ds(src_set * toks + start, 4)],
             bufs[a].at[pl.ds(dst_set * toks + start, 4)],
-            z_send.at[a, hop, gi], z_recv.at[a, hop, gi], (dev, me),
+            z_send.at[a, hop, gi], z_recv.at[a, hop, gi], dev,
         )
 
     stage_array(0)
@@ -190,7 +201,7 @@
             z_copy(1, hop, gi, GX[gi]).wait_recv()
 
     def o_copy(t):
-        return remote(obuf.at[t], orecv.at[me], o_send.at[t], o_recv.at[me], (view, t))
+        return remote(obuf.at[t], orecv.at[unit_of(me)], o_send.at[t], o_recv.at[me], (view, t))
 
     def sum_tile(d, carry):
         t = lax.rem(me + 1 + d, toks)
@@ -207,11 +218,11 @@
         return carry
 
     lax.fori_loop(0, 16, sum_tile, 0)
-    orecv[me] = obuf[me]
+    orecv[unit_of(me)] = obuf[me]
 
     for d in range(1, 16):
         src = lax.rem(me + toks - d, toks)
-        remote(obuf.at[0], orecv.at[src], o_send.at[0], o_recv.at[src], (view, src)).wait_recv()
+        remote(obuf.at[0], orecv.at[unit_of(src)], o_send.at[0], o_recv.at[src], (view, src)).wait_recv()
     for s in range(2):
         role = first_slot if s == 0 else 1 - first_slot
         for p in range(8):

time: 140 us -> 86.4 us (0.62); the launches traced: 138 us -> 86.1 us
  Pallas kernels: 133 us -> 81.3 us
    pallas_call x1, Pallas kernels: 133 us -> 81.3 us  [local(): pl.pallas_call(attend_kernel, out_shape=jax.ShapeDtypeStruct(queries.shap...]
where the time goes in v2:
time: 86.4 us; the launch traced here: 86.1 us
  Pallas kernels  81.3 us (94%)
  local copies, waits for them, and re-layouts  4.7 us (5%)
    pallas_call x1, Pallas kernels, local(): pl.pallas_call(attend_kernel, out_shape=jax.ShapeDtypeStruct(queries.shap...  81.3 us
    unnamed x12, local copies, waits for them, and re-layouts  4.7 us

profile of v2, /device:TPU:1, one launch (start us, length us, event | category | flops | bytes accessed | tf_op | source)
XLA Modules:
  0.0 86.1 jit_solution(9764047494867915480)
XLA Ops:
  0.0 0.0 copy-start.4
  0.0 0.0 copy-start.3
  0.0 0.8 copy.7.slot_ref
  0.8 0.0 copy-done.4
  0.8 0.0 copy-done.3
  0.8 0.0 copy-start
  0.8 1.0 %copy-done = bf16[1,2,128,1024]{3,2,1,0:T(8,128)(2,1)S(1)} copy-done((bf16[1,2,128,1024]{3,2,1,0:T(8,128)(2,1)S(1)}, bf16[1,2,128,1024]{3,2,1,0:T(8,128)(2,1)}, u32[]{:S(2)}) %copy-start) | copy-done | bytes 524312
  1.8 0.0 copy-start.1
  1.8 1.0 %copy-done.1 = bf16[1,2,128,1024]{3,2,1,0:T(8,128)(2,1)S(1)} copy-done((bf16[1,2,128,1024]{3,2,1,0:T(8,128)(2,1)S(1)}, bf16[1,2,128,1024]{3,2,1,0:T(8,128)(2,1)}, u32[]{:S(2)}) %copy-start.1) | copy-done | bytes 524312
  2.9 0.0 copy-start.2
  2.9 1.0 %copy-done.2 = bf16[1,2,128,1024]{3,2,1,0:T(8,128)(2,1)S(1)} copy-done((bf16[1,2,128,1024]{3,2,1,0:T(8,128)(2,1)S(1)}, bf16[1,2,128,1024]{3,2,1,0:T(8,128)(2,1)}, u32[]{:S(2)}) %copy-start.2) | copy-done | bytes 524312
  3.9 81.3 %shard_map.64 = bf16[1,2,128,1024]{3,2,1,0:T(8,128)(2,1)S(1)} custom-call(s32[1,2,16,16]{3,2,1,0:T(8,128)S(1)} %copy-done.3, s32[1,2]{1,0:T(1,128)S(1)} %copy-done.4, s32[32,2]{1,0:T(8,128)S(1)} %copy.7.slot_ref, bf16[1,2,128,1024]{3,2,1,0:T(8,128)(2,1)S(1)} %copy-done, bf16[1,2,128,1024]{3,2,1,0:T(8,128)(2,1)S(1)} %copy-done.1, ...), custom_call_target="tpu_custom_call" | custom-call | flops 3500000000 | bytes 2097152 | tf_op jit(solution)/shard_map/pallas_call | solution.py:249
  85.3 0.8 copy.9
Async XLA Ops:
  0.0 0.8 copy-start.4
  0.0 0.8 copy-start.3
  0.8 1.0 %copy-start = (bf16[1,2,128,1024]{3,2,1,0:T(8,128)(2,1)S(1)}, bf16[1,2,128,1024]{3,2,1,0:T(8,128)(2,1)}, u32[]{:S(2)}) copy-start(bf16[1,2,128,1024]{3,2,1,0:T(8,128)(2,1)} %q_ref.1) | copy-start | bytes 1572868
  1.8 1.0 %copy-start.1 = (bf16[1,2,128,1024]{3,2,1,0:T(8,128)(2,1)S(1)}, bf16[1,2,128,1024]{3,2,1,0:T(8,128)(2,1)}, u32[]{:S(2)}) copy-start(bf16[1,2,128,1024]{3,2,1,0:T(8,128)(2,1)} %k_ref.1) | copy-start | bytes 1572868
  2.9 1.0 %copy-start.2 = (bf16[1,2,128,1024]{3,2,1,0:T(8,128)(2,1)S(1)}, bf16[1,2,128,1024]{3,2,1,0:T(8,128)(2,1)}, u32[]{:S(2)}) copy-start(bf16[1,2,128,1024]{3,2,1,0:T(8,128)(2,1)} %v_ref.1) | copy-start | bytes 1572868

commit v3 on v2

v3 whole, which is shorter than its diff:
```python
import jax
import jax.numpy as jnp
from jax import lax
from jax.experimental import pallas as pl
from jax.experimental.pallas import tpu as pltpu
from jax.sharding import PartitionSpec as P

MESH = pl.DeviceIdType.MESH
TILE = 128
LANES = 128
HD = 64
BAND = 6
NB = 2
KEY_COLS = 1 + NB * BAND
NEG_SCORE = -1e30
VMEM_BYTES = 63 * 1024 * 1024
XS = 4
ROWS = 64
LOW_STEP = 1
HIGH_STEP = 11
GX = (0, 1, 3, 2)


def attend_kernel(
    mask_ref, off_ref, slot_ref, q_ref, k_ref, v_ref, out_ref,
    raw_k, raw_v, raw_q, stage_k, stage_v, stage_q, qbuf, kbuf, vown, vlow, vhigh, vun_low, vun_high, sbuf, wbuf,
    obuf, orecv, start_s, count_s,
    in_sem, a_send, a_recv, z_send, z_recv, o_send, o_recv,
):
    views = lax.axis_size("view")
    toks = lax.axis_size("tok")
    group = toks // XS
    view = lax.axis_index("view")
    me = lax.axis_index("tok")
    right = lax.rem(view + 1, views)
    left = lax.rem(view + views - 1, views)
    my_x = me // group
    my_r = lax.rem(me, group)
    half = views // 2
    upper = view // half

    def flip(tok, by):
        return tok + by * (2 - 4 * lax.rem(tok // 2, 2))

    def unit_of(tok):
        return flip(tok, upper)

    right_dev = (right, flip(me, lax.rem(upper + right // half, 2)))
    left_dev = (left, flip(me, lax.rem(upper + left // half, 2)))
    raws = (raw_k, raw_v, raw_q)
    stages = (stage_k, stage_v, stage_q)
    bufs = (kbuf, vown, qbuf)

    def remote(src, dst, send, recv, dev):
        return pltpu.make_async_remote_copy(
            src_ref=src, dst_ref=dst, send_sem=send, recv_sem=recv, device_id=dev, device_id_type=MESH
        )

    def in_copy(a):
        return pltpu.make_async_copy((k_ref, v_ref, q_ref)[a].at[0], raws[a], in_sem.at[a])

    for a in range(3):
        in_copy(a).start()

    barrier = pltpu.get_barrier_semaphore()
    for to in (right_dev, left_dev):
        pl.semaphore_signal(barrier, inc=1, device_id=to, device_id_type=MESH)
    for d in range(1, 16):
        pl.semaphore_signal(barrier, inc=1, device_id=(view, lax.rem(me + d, toks)), device_id_type=MESH)

    first_slot = slot_ref[0, view]

    def swap_halves(x, y):
        return (
            jnp.concatenate([x[:, :HD], y[:, :HD]], axis=1),
            jnp.concatenate([x[:, HD:], y[:, HD:]], axis=1),
        )

    def stage_array(a):
        in_copy(a).wait()
        for b in range(2):
            slot = first_slot if b == 0 else 1 - first_slot
            for p in range(8):
                tile = raws[a][slot, :, p * LANES:(p + 1) * LANES]
                if a == 1:
                    low_head, high_head = swap_halves(tile[:HD], tile[HD:])
                    stage_v[p * 2 + b, 0] = low_head
                    stage_v[p * 2 + b, 1] = high_head
                else:
                    stages[a][p * 2 + b] = tile
        bufs[a][me] = stages[a][unit_of(me)]

    def a2a_copy(a, dest):
        return remote(stages[a].at[unit_of(dest)], bufs[a].at[me], a_send.at[a, dest], a_recv.at[a, me], (view, dest))

    def a2a_send(a, columns=GX):
        for gx in columns:
            for r in range(4):
                if (gx, r) != (0, 0):
                    dest = lax.rem(my_x + gx, XS) * group + lax.rem(my_r + r, group)
                    a2a_copy(a, dest).start()

    def a2a_wait(a, gx):
        for r in range(4):
            if (gx, r) != (0, 0):
                src = lax.rem(my_x + XS - gx, XS) * group + lax.rem(my_r + group - r, group)
                remote(stages[a].at[0], bufs[a].at[src], a_send.at[a, 0], a_recv.at[a, src], (view, src)).wait_recv()

    def z_copy(a, hop, gi, gx):
        start = lax.rem(my_x + XS - gx, XS) * group
        src_set, dst_set, dev = ((0, 1, right_dev), (0, 2, left_dev), (1, 3, right_dev), (2, 4, left_dev))[hop]
        if a == 0:
            src = kbuf.at[pl.ds(src_set * toks + start, 4)]
            dst = kbuf.at[pl.ds(dst_set * toks + start, 4)]
        else:
            buf = (vlow, vhigh)[a - 1]
            if hop < 2:
                src = vown.at[pl.ds(start, 4), a - 1]
            else:
                src = buf.at[pl.ds((src_set - 1) * toks + start, 4)]
            dst = buf.at[pl.ds((dst_set - 1) * toks + start, 4)]
        return remote(src, dst, z_send.at[a, hop, gi], z_recv.at[a, hop, gi], dev)

    def send_own(a, gi, gx):
        for hop in (0, 1):
            z_copy(a, hop, gi, gx).start()

    def send_on(a, gi, gx):
        for hop in (0, 1):
            z_copy(a, hop, gi, gx).wait_recv()
            z_copy(a, hop + 2, gi, gx).start()

    def wait_far(a):
        for gi in range(4):
            for hop in (2, 3):
                z_copy(a, hop, gi, GX[gi]).wait_recv()

    stage_array(0)
    pl.semaphore_wait(barrier, 17)
    a2a_send(0, (0,))
    a2a_send(0, (1, 3))
    a2a_wait(0, 0)
    send_own(0, 0, 0)
    a2a_send(0, (2,))
    stage_array(1)
    for gi in (1, 2):
        a2a_wait(0, GX[gi])
        send_own(0, gi, GX[gi])
    stage_array(2)
    a2a_send(1)
    a2a_send(2)
    a2a_wait(0, GX[3])
    send_own(0, 3, GX[3])
    for gi in range(4):
        send_on(0, gi, GX[gi])
    for gi in range(4):
        a2a_wait(1, GX[gi])
        send_own(1, gi, GX[gi])

    for j in range(NB):
        def count_row(t, carry, j=j):
            first = jnp.int32(0)
            total = jnp.int32(0)
            before = mask_ref[0, j, t, 15]
            for k in range(16):
                here = mask_ref[0, j, t, k]
                total = total + here
                first = first + jnp.where((here == 1) & (before == 0), k, 0)
                before = here
            start_s[j, t] = first
            count_s[j, t] = total
            return carry
        lax.fori_loop(0, 16, count_row, 0)

    for gx in GX:
        a2a_wait(2, gx)
    wait_far(0)

    sets = []
    for j in range(NB):
        off = off_ref[0, j]
        sets.append(jnp.where(off == -1, 1, jnp.where(off == 1, 2, jnp.where(off == -2, 3, 4))) * toks)
    low = lax.broadcasted_iota(jnp.int32, (TILE, LANES), 1) < HD

    def paired(j, t, i):
        return lax.rem(start_s[j, t] + i, 16)

    def dot_t(x, y):
        return lax.dot_general(x, y, (((1,), (1,)), ((), ())), preferred_element_type=jnp.float32)

    def weigh_tile(t):
        q = qbuf[t] * jnp.bfloat16(0.125)
        zero = jnp.zeros_like(q)
        both = jnp.concatenate([jnp.where(low, q, zero), jnp.where(low, zero, q)], axis=0)
        sbuf[:, :LANES] = dot_t(both, kbuf[t])
        for j in range(NB):
            for i in range(0, BAND, 2):
                keys = jnp.concatenate(
                    [kbuf[sets[j] + paired(j, t, i)], kbuf[sets[j] + paired(j, t, i + 1)]], axis=0
                )
                s = dot_t(both, keys)
                for h in range(2):
                    bias = jnp.where(i + h < count_s[j, t], jnp.float32(0), jnp.float32(NEG_SCORE))
                    c = 1 + j * BAND + i + h
                    sbuf[:, c * LANES:(c + 1) * LANES] = s[:, h * LANES:(h + 1) * LANES] + bias
        for rb in range(0, 2 * TILE, ROWS):
            rows = pl.ds(rb, ROWS)
            top = sbuf[rows, :LANES]
            for c in range(1, KEY_COLS):
                top = jnp.maximum(top, sbuf[rows, c * LANES:(c + 1) * LANES])
            top = jnp.max(top, axis=1, keepdims=True)
            total = jnp.zeros((ROWS, LANES), jnp.float32)
            for c in range(KEY_COLS):
                e = jnp.exp(sbuf[rows, c * LANES:(c + 1) * LANES] - top)
                sbuf[rows, c * LANES:(c + 1) * LANES] = e
                total = total + e
            inv = 1.0 / jnp.sum(total, axis=1, keepdims=True)
            for c in range(KEY_COLS):
                wbuf[t, rows, c * LANES:(c + 1) * LANES] = (
                    sbuf[rows, c * LANES:(c + 1) * LANES] * inv
                ).astype(jnp.bfloat16)

    def gx_of(gi):
        return gi + (gi // 2) * (1 - 2 * lax.rem(gi, 2))

    def weigh_step(t, carry):
        weigh_tile(t)

        @pl.when((t >= LOW_STEP) & (t < LOW_STEP + 4))
        def _():
            gi = t - LOW_STEP
            send_on(1, gi, gx_of(gi))
            send_own(2, gi, gx_of(gi))

        @pl.when((t >= HIGH_STEP) & (t < HIGH_STEP + 4))
        def _():
            gi = t - HIGH_STEP
            send_on(2, gi, gx_of(gi))

        return carry

    lax.fori_loop(0, 16, weigh_step, 0)

    def o_copy(h, t):
        return remote(obuf.at[h, t], orecv.at[h, unit_of(me)], o_send.at[h, t], o_recv.at[h, me], (view, t))

    for h in range(2):
        wait_far(1 + h)
        buf = (vlow, vhigh)[h]
        vun = (vun_low, vun_high)[h]

        def unpack(t, carry, h=h, buf=buf, vun=vun):
            for n in range(1 + NB):
                pack = vown[t, h] if n == 0 else buf[sets[n - 1] - toks + t]
                vun[n * 16 + t, :HD] = pack
                vun[n * 16 + t, HD:] = jnp.concatenate([pack[:, HD:], pack[:, :HD]], axis=1)
            return carry

        lax.fori_loop(0, 16, unpack, 0)

        def sum_tiles(d, carry, h=h, vun=vun):
            ts = [lax.rem(me + 1 + 4 * d + n, toks) for n in range(4)]
            for t in ts:
                parts = [vun[t]]
                for j in range(NB):
                    parts += [vun[16 * (1 + j) + paired(j, t, i)] for i in range(BAND)]
                acc = jnp.dot(
                    wbuf[t, h * TILE:(h + 1) * TILE], jnp.concatenate(parts, axis=0),
                    preferred_element_type=jnp.float32,
                )
                obuf[h, t] = jnp.concatenate([acc[:HD, :HD], acc[HD:, :HD]], axis=1).astype(jnp.bfloat16)
            for t in ts:
                @pl.when(t != me)
                def _(t=t):
                    o_copy(h, t).start()

            return carry

        lax.fori_loop(0, 4, sum_tiles, 0)
        orecv[h, unit_of(me)] = obuf[h, me]

    for h in range(2):
        for d in range(1, 16):
            src = lax.rem(me + toks - d, toks)
            remote(obuf.at[0, 0], orecv.at[h, unit_of(src)], o_send.at[h, 0], o_recv.at[h, src], (view, src)).wait_recv()
    for s in range(2):
        role = first_slot if s == 0 else 1 - first_slot
        for p in range(8):
            upper_rows, lower_rows = swap_halves(orecv[0, p * 2 + role], orecv[1, p * 2 + role])
            out_ref[0, s, :HD, p * LANES:(p + 1) * LANES] = upper_rows
            out_ref[0, s, HD:, p * LANES:(p + 1) * LANES] = lower_rows

    for d in range(1, 16):
        peer = lax.rem(me + d, toks)
        for a in range(3):
            a2a_copy(a, peer).wait_send()
        for h in range(2):
            o_copy(h, peer).wait_send()
    for a in range(3):
        for hop in range(4):
            for gi in range(4):
                z_copy(a, hop, gi, GX[gi]).wait_send()


def local(queries, keys, values, tile_mask, offsets, branch_slots):
    bf16 = jnp.bfloat16
    smem = pl.BlockSpec(memory_space=pltpu.SMEM)
    hbm = pl.BlockSpec(memory_space=pl.ANY)
    dma = pltpu.SemaphoreType.DMA
    return pl.pallas_call(
        attend_kernel,
        out_shape=jax.ShapeDtypeStruct(queries.shape, bf16),
        in_specs=[smem, smem, smem, hbm, hbm, hbm],
        out_specs=pl.BlockSpec(memory_space=pltpu.VMEM),
        scratch_shapes=[
            pltpu.VMEM((2, TILE, 1024), bf16),
            pltpu.VMEM((2, TILE, 1024), bf16),
            pltpu.VMEM((2, TILE, 1024), bf16),
            pltpu.VMEM((16, TILE, LANES), bf16),
            pltpu.VMEM((16, 2, HD, LANES), bf16),
            pltpu.VMEM((16, TILE, LANES), bf16),
            pltpu.VMEM((16, TILE, LANES), bf16),
            pltpu.VMEM((80, TILE, LANES), bf16),
            pltpu.VMEM((16, 2, HD, LANES), bf16),
            pltpu.VMEM((64, HD, LANES), bf16),
            pltpu.VMEM((64, HD, LANES), bf16),
            pltpu.VMEM((48, TILE, LANES), bf16),
            pltpu.VMEM((48, TILE, LANES), bf16),
            pltpu.VMEM((2 * TILE, KEY_COLS * LANES), jnp.float32),
            pltpu.VMEM((16, 2 * TILE, KEY_COLS * LANES), bf16),
            pltpu.VMEM((2, 16, HD, LANES), bf16),
            pltpu.VMEM((2, 16, HD, LANES), bf16),
            pltpu.SMEM((NB, 16), jnp.int32),
            pltpu.SMEM((NB, 16), jnp.int32),
            dma((3,)),
            dma((3, 16)),
            dma((3, 16)),
            dma((3, 4, 4)),
            dma((3, 4, 4)),
            dma((2, 16)),
            dma((2, 16)),
        ],
        compiler_params=pltpu.CompilerParams(
            collective_id=0, has_side_effects=True, vmem_limit_bytes=VMEM_BYTES
        ),
        cost_estimate=pl.CostEstimate(flops=3_500_000_000, bytes_accessed=2 << 20, transcendentals=7_000_000),
    )(tile_mask, offsets, branch_slots.T, queries, keys, values)


def solution(mesh):
    in_specs = (
        P("view", None, "tok", None),
        P("view", None, "tok", None),
        P("view", None, "tok", None),
        P("view", None, None, None),
        P("view", None),
        P(),
    )
    out_specs = P("view", None, "tok", None)
    return jax.shard_map(local, mesh=mesh, in_specs=in_specs, out_specs=out_specs, check_vma=False)
```

time: 86.4 us -> 82.2 us (0.951)
  local copies, waits for them, and re-layouts: 4.7 us -> 1.87 us
  Pallas kernels: 81.3 us -> 80.1 us
    unnamed x12 -> x1, local copies, waits for them, and re-layouts: 4.7 us -> 1.87 us
    pallas_call x1, Pallas kernels: 81.3 us -> 80.1 us  [local(): pl.pallas_call(attend_kernel, out_shape=jax.ShapeDtypeStruct(queries.shap...]
where the time goes in v3:
time: 82.2 us; the launch traced here: 82 us
  Pallas kernels  80.1 us (97%)
  local copies, waits for them, and re-layouts  1.87 us (2%)
    pallas_call x1, Pallas kernels, local(): pl.pallas_call(attend_kernel, out_shape=jax.ShapeDtypeStruct(queries.shap...  80.1 us
    unnamed x1, local copies, waits for them, and re-layouts  1.87 us

profile of v3, /device:TPU:1, one launch (start us, length us, event | category | flops | bytes accessed | tf_op | source)
XLA Modules:
  0.0 82.0 jit_solution(16300876087672146079)
XLA Ops:
  0.0 80.1 %shard_map.64 = bf16[1,2,128,1024]{3,2,1,0:T(8,128)(2,1)} custom-call(s32[1,2,16,16]{3,2,1,0:T(8,128)} %mask_ref.1, s32[1,2]{1,0:T(1,128)} %off_ref.1, s32[2,32]{1,0:T(2,128)} %bitcast.1, bf16[1,2,128,1024]{3,2,1,0:T(8,128)(2,1)} %q_ref.1, bf16[1,2,128,1024]{3,2,1,0:T(8,128)(2,1)} %k_ref.1, bf16[1,2,128,1024]{3,2,1,0:T(8,128)(2,1)} %v_ref.1), custom_call_target="tpu_custom_call" | custom-call | flops 3500000000 | bytes 2097152 | tf_op jit(solution)/shard_map/pallas_call | solution.py:310
  80.1 1.9 %copy.8 = bf16[1,2,128,1024]{3,2,1,0:T(8,128)(2,1)} copy(bf16[1,2,128,1024]{3,2,1,0:T(8,128)(2,1)} %shard_map.64) | data formatting | bytes 1048576

commit v4 on v3

--- a/solution.py
+++ b/solution.py
@@ -22,8 +22,9 @@
 
 
 def attend_kernel(
-    mask_ref, off_ref, slot_ref, q_ref, k_ref, v_ref, out_ref,
-    raw_k, raw_v, raw_q, stage_k, stage_v, stage_q, qbuf, kbuf, vown, vlow, vhigh, vun_low, vun_high, sbuf, wbuf,
+    mask_in, off_in, slot_in, q_ref, k_ref, v_ref, out_ref,
+    mask_ref, off_ref, slot_ref,
+    raw_k, raw_v, raw_q, stage_k, stage_v, stage_q, qbuf, kbuf, vown, vlow, vhigh, own_sum, sbuf, wbuf,
     obuf, orecv, start_s, count_s,
     in_sem, a_send, a_recv, z_send, z_recv, o_send, o_recv,
 ):
@@ -59,8 +60,15 @@
     def in_copy(a):
         return pltpu.make_async_copy((k_ref, v_ref, q_ref)[a].at[0], raws[a], in_sem.at[a])
 
+    tables = [
+        pltpu.make_async_copy(src, dst, in_sem.at[3 + n])
+        for n, (src, dst) in enumerate(((slot_in, slot_ref), (off_in, off_ref), (mask_in, mask_ref)))
+    ]
+    tables[0].start()
     for a in range(3):
         in_copy(a).start()
+    for table in tables[1:]:
+        table.start()
 
     barrier = pltpu.get_barrier_semaphore()
     for to in (right_dev, left_dev):
@@ -68,6 +76,7 @@
     for d in range(1, 16):
         pl.semaphore_signal(barrier, inc=1, device_id=(view, lax.rem(me + d, toks)), device_id_type=MESH)
 
+    tables[0].wait()
     first_slot = slot_ref[0, view]
 
     def swap_halves(x, y):
@@ -93,17 +102,20 @@
     def a2a_copy(a, dest):
         return remote(stages[a].at[unit_of(dest)], bufs[a].at[me], a_send.at[a, dest], a_recv.at[a, me], (view, dest))
 
+    def mate(r, n):
+        other = r + 1 - 2 * lax.rem(r, 2) if n % 2 else r
+        return lax.rem(other + 2, group) if n >= 2 else other
+
     def a2a_send(a, columns=GX):
         for gx in columns:
-            for r in range(4):
-                if (gx, r) != (0, 0):
-                    dest = lax.rem(my_x + gx, XS) * group + lax.rem(my_r + r, group)
-                    a2a_copy(a, dest).start()
-
-    def a2a_wait(a, gx):
-        for r in range(4):
-            if (gx, r) != (0, 0):
-                src = lax.rem(my_x + XS - gx, XS) * group + lax.rem(my_r + group - r, group)
+            for n in range(4):
+                if (gx, n) != (0, 0):
+                    a2a_copy(a, lax.rem(my_x + gx, XS) * group + mate(my_r, n)).start()
+
+    def a2a_wait(a, gx, mates=range(4)):
+        for n in mates:
+            if (gx, n) != (0, 0):
+                src = lax.rem(my_x + XS - gx, XS) * group + mate(my_r, n)
                 remote(stages[a].at[0], bufs[a].at[src], a_send.at[a, 0], a_recv.at[a, src], (view, src)).wait_recv()
 
     def z_copy(a, hop, gi, gx):
@@ -119,7 +131,28 @@
             else:
                 src = buf.at[pl.ds((src_set - 1) * toks + start, 4)]
             dst = buf.at[pl.ds((dst_set - 1) * toks + start, 4)]
-        return remote(src, dst, z_send.at[a, hop, gi], z_recv.at[a, hop, gi], dev)
+        sem = gi + 3 if a == 0 else gi
+        return remote(src, dst, z_send.at[a, hop, sem], z_recv.at[a, hop, sem], dev)
+
+    def unit_place(by):
+        return lax.rem(flip(me, lax.rem(upper + lax.rem(view + views + by, views) // half, 2)), group)
+
+    def z_tile(hop, n, origin):
+        tile = my_x * group + mate(unit_place(origin), n)
+        src_set, dst_set, dev = ((0, 1, right_dev), (0, 2, left_dev), (1, 3, right_dev), (2, 4, left_dev))[hop]
+        return remote(
+            kbuf.at[src_set * toks + tile], kbuf.at[dst_set * toks + tile],
+            z_send.at[0, hop, n], z_recv.at[0, hop, n], dev,
+        )
+
+    def send_tile(n):
+        for hop in (0, 1):
+            z_tile(hop, n, 0).start()
+
+    def send_tile_on(n):
+        for hop, origin in ((0, -1), (1, 1)):
+            z_tile(hop, n, origin).wait_recv()
+            z_tile(hop + 2, n, origin).start()
 
     def send_own(a, gi, gx):
         for hop in (0, 1):
@@ -131,16 +164,22 @@
             z_copy(a, hop + 2, gi, gx).start()
 
     def wait_far(a):
-        for gi in range(4):
+        if a == 0:
+            for n in range(4):
+                for hop, origin in ((2, -2), (3, 2)):
+                    z_tile(hop, n, origin).wait_recv()
+        for gi in range(1 if a == 0 else 0, 4):
             for hop in (2, 3):
                 z_copy(a, hop, gi, GX[gi]).wait_recv()
 
     stage_array(0)
     pl.semaphore_wait(barrier, 17)
+    send_tile(0)
     a2a_send(0, (0,))
     a2a_send(0, (1, 3))
-    a2a_wait(0, 0)
-    send_own(0, 0, 0)
+    for n in range(1, 4):
+        a2a_wait(0, 0, (n,))
+        send_tile(n)
     a2a_send(0, (2,))
     stage_array(1)
     for gi in (1, 2):
@@ -151,11 +190,16 @@
     a2a_send(2)
     a2a_wait(0, GX[3])
     send_own(0, 3, GX[3])
-    for gi in range(4):
+    for n in range(4):
+        send_tile_on(n)
+    for gi in range(1, 4):
         send_on(0, gi, GX[gi])
     for gi in range(4):
         a2a_wait(1, GX[gi])
         send_own(1, gi, GX[gi])
+
+    for table in tables[1:]:
+        table.wait()
 
     for j in range(NB):
         def count_row(t, carry, j=j):
@@ -181,6 +225,10 @@
         off = off_ref[0, j]
         sets.append(jnp.where(off == -1, 1, jnp.where(off == 1, 2, jnp.where(off == -2, 3, 4))) * toks)
     low = lax.broadcasted_iota(jnp.int32, (TILE, LANES), 1) < HD
+    low_row = lax.broadcasted_iota(jnp.int32, (1, LANES), 1) < HD
+
+    def roll_half(x):
+        return jnp.concatenate([x[:, HD:], x[:, :HD]], axis=1)
 
     def paired(j, t, i):
         return lax.rem(start_s[j, t] + i, 16)
@@ -195,13 +243,15 @@
         sbuf[:, :LANES] = dot_t(both, kbuf[t])
         for j in range(NB):
             for i in range(0, BAND, 2):
-                keys = jnp.concatenate(
-                    [kbuf[sets[j] + paired(j, t, i)], kbuf[sets[j] + paired(j, t, i + 1)]], axis=0
+                one, two = kbuf[sets[j] + paired(j, t, i)], kbuf[sets[j] + paired(j, t, i + 1)]
+                s = dot_t(both, jnp.concatenate([one[:HD], two[:HD], one[HD:], two[HD:]], axis=0))
+                bias = jnp.where(
+                    low_row,
+                    jnp.where(i < count_s[j, t], jnp.float32(0), jnp.float32(NEG_SCORE)),
+                    jnp.where(i + 1 < count_s[j, t], jnp.float32(0), jnp.float32(NEG_SCORE)),
                 )
-                s = dot_t(both, keys)
                 for h in range(2):
-                    bias = jnp.where(i + h < count_s[j, t], jnp.float32(0), jnp.float32(NEG_SCORE))
-                    c = 1 + j * BAND + i + h
+                    c = 1 + h * BAND + (j * BAND + i) // 2
                     sbuf[:, c * LANES:(c + 1) * LANES] = s[:, h * LANES:(h + 1) * LANES] + bias
         for rb in range(0, 2 * TILE, ROWS):
             rows = pl.ds(rb, ROWS)
@@ -219,6 +269,13 @@
                 wbuf[t, rows, c * LANES:(c + 1) * LANES] = (
                     sbuf[rows, c * LANES:(c + 1) * LANES] * inv
                 ).astype(jnp.bfloat16)
+        for h in range(2):
+            pack = vown[t, h]
+            part = jnp.dot(
+                wbuf[t, h * TILE:(h + 1) * TILE, :LANES], jnp.concatenate([pack, roll_half(pack)], axis=0),
+                preferred_element_type=jnp.float32,
+            )
+            own_sum[h, t] = jnp.concatenate([part[:HD, :HD], part[HD:, :HD]], axis=1)
 
     def gx_of(gi):
         return gi + (gi // 2) * (1 - 2 * lax.rem(gi, 2))
@@ -247,28 +304,22 @@
     for h in range(2):
         wait_far(1 + h)
         buf = (vlow, vhigh)[h]
-        vun = (vun_low, vun_high)[h]
-
-        def unpack(t, carry, h=h, buf=buf, vun=vun):
-            for n in range(1 + NB):
-                pack = vown[t, h] if n == 0 else buf[sets[n - 1] - toks + t]
-                vun[n * 16 + t, :HD] = pack
-                vun[n * 16 + t, HD:] = jnp.concatenate([pack[:, HD:], pack[:, :HD]], axis=1)
-            return carry
-
-        lax.fori_loop(0, 16, unpack, 0)
-
-        def sum_tiles(d, carry, h=h, vun=vun):
+
+        def sum_tiles(d, carry, h=h, buf=buf):
             ts = [lax.rem(me + 1 + 4 * d + n, toks) for n in range(4)]
             for t in ts:
-                parts = [vun[t]]
+                parts = []
                 for j in range(NB):
-                    parts += [vun[16 * (1 + j) + paired(j, t, i)] for i in range(BAND)]
-                acc = jnp.dot(
-                    wbuf[t, h * TILE:(h + 1) * TILE], jnp.concatenate(parts, axis=0),
-                    preferred_element_type=jnp.float32,
-                )
-                obuf[h, t] = jnp.concatenate([acc[:HD, :HD], acc[HD:, :HD]], axis=1).astype(jnp.bfloat16)
+                    parts += [buf[sets[j] - toks + paired(j, t, i)] for i in range(BAND)]
+                weights = wbuf.at[t, pl.ds(h * TILE, TILE)]
+                cut = (1 + BAND) * LANES
+                both = jnp.concatenate([weights[:, LANES:cut], weights[:, cut:]], axis=0)
+                acc = jnp.dot(both, jnp.concatenate(parts, axis=0), preferred_element_type=jnp.float32)
+                first, second = acc[:TILE], acc[TILE:]
+                obuf[h, t] = (
+                    own_sum[h, t]
+                    + jnp.where(low[:HD], first[:HD] + roll_half(second[:HD]), roll_half(first[HD:]) + second[HD:])
+                ).astype(jnp.bfloat16)
             for t in ts:
                 @pl.when(t != me)
                 def _(t=t):
@@ -296,23 +347,28 @@
             a2a_copy(a, peer).wait_send()
         for h in range(2):
             o_copy(h, peer).wait_send()
+    for n in range(4):
+        for hop, origin in ((0, 0), (1, 0), (2, -1), (3, 1)):
+            z_tile(hop, n, origin).wait_send()
     for a in range(3):
         for hop in range(4):
-            for gi in range(4):
+            for gi in range(1 if a == 0 else 0, 4):
                 z_copy(a, hop, gi, GX[gi]).wait_send()
 
 
 def local(queries, keys, values, tile_mask, offsets, branch_slots):
     bf16 = jnp.bfloat16
-    smem = pl.BlockSpec(memory_space=pltpu.SMEM)
     hbm = pl.BlockSpec(memory_space=pl.ANY)
     dma = pltpu.SemaphoreType.DMA
     return pl.pallas_call(
         attend_kernel,
         out_shape=jax.ShapeDtypeStruct(queries.shape, bf16),
-        in_specs=[smem, smem, smem, hbm, hbm, hbm],
+        in_specs=[hbm] * 6,
         out_specs=pl.BlockSpec(memory_space=pltpu.VMEM),
         scratch_shapes=[
+            pltpu.SMEM((1, NB, 16, 16), jnp.int32),
+            pltpu.SMEM((1, NB), jnp.int32),
+            pltpu.SMEM((2, 32), jnp.int32),
             pltpu.VMEM((2, TILE, 1024), bf16),
             pltpu.VMEM((2, TILE, 1024), bf16),
             pltpu.VMEM((2, TILE, 1024), bf16),
@@ -324,19 +380,18 @@
             pltpu.VMEM((16, 2, HD, LANES), bf16),
             pltpu.VMEM((64, HD, LANES), bf16),
             pltpu.VMEM((64, HD, LANES), bf16),
-            pltpu.VMEM((48, TILE, LANES), bf16),
-            pltpu.VMEM((48, TILE, LANES), bf16),
+            pltpu.VMEM((2, 16, HD, LANES), jnp.float32),
             pltpu.VMEM((2 * TILE, KEY_COLS * LANES), jnp.float32),
             pltpu.VMEM((16, 2 * TILE, KEY_COLS * LANES), bf16),
             pltpu.VMEM((2, 16, HD, LANES), bf16),
             pltpu.VMEM((2, 16, HD, LANES), bf16),
             pltpu.SMEM((NB, 16), jnp.int32),
             pltpu.SMEM((NB, 16), jnp.int32),
-            dma((3,)),
+            dma((6,)),
             dma((3, 16)),
             dma((3, 16)),
-            dma((3, 4, 4)),
-            dma((3, 4, 4)),
+            dma((3, 4, 7)),
+            dma((3, 4, 7)),
             dma((2, 16)),
             dma((2, 16)),
         ],

time: 82.2 us -> 77.9 us (0.948)
  Pallas kernels: 80.1 us -> 75.8 us
    pallas_call x1, Pallas kernels: 80.1 us -> 75.8 us  [local(): pl.pallas_call(attend_kernel, out_shape=jax.ShapeDtypeStruct(queries.shap...]
where the time goes in v4:
time: 77.9 us; the launch traced here: 77.7 us
  Pallas kernels  75.8 us (97%)
  local copies, waits for them, and re-layouts  1.87 us (2%)
    pallas_call x1, Pallas kernels, local(): pl.pallas_call(attend_kernel, out_shape=jax.ShapeDtypeStruct(queries.shap...  75.8 us
    unnamed x1, local copies, waits for them, and re-layouts  1.87 us

profile of v4, /device:TPU:1, one launch (start us, length us, event | category | flops | bytes accessed | tf_op | source)
XLA Modules:
  0.0 77.7 jit_solution(11408455205134722210)
XLA Ops:
  0.0 75.8 %shard_map.64 = bf16[1,2,128,1024]{3,2,1,0:T(8,128)(2,1)} custom-call(s32[1,2,16,16]{3,2,1,0:T(8,128)} %mask_in.1, s32[1,2]{1,0:T(1,128)} %off_in.1, s32[2,32]{1,0:T(2,128)} %bitcast.1, bf16[1,2,128,1024]{3,2,1,0:T(8,128)(2,1)} %q_ref.1, bf16[1,2,128,1024]{3,2,1,0:T(8,128)(2,1)} %k_ref.1, bf16[1,2,128,1024]{3,2,1,0:T(8,128)(2,1)} %v_ref.1), custom_call_target="tpu_custom_call" | custom-call | flops 3500000000 | bytes 2097152 | tf_op jit(solution)/shard_map/pallas_call | solution.py:363
  75.8 1.9 %copy.8 = bf16[1,2,128,1024]{3,2,1,0:T(8,128)(2,1)} copy(bf16[1,2,128,1024]{3,2,1,0:T(8,128)(2,1)} %shard_map.64) | data formatting | bytes 1048576

commit v5 on v4

--- a/solution.py
+++ b/solution.py
@@ -99,24 +99,38 @@
                     stages[a][p * 2 + b] = tile
         bufs[a][me] = stages[a][unit_of(me)]
 
-    def a2a_copy(a, dest):
-        return remote(stages[a].at[unit_of(dest)], bufs[a].at[me], a_send.at[a, dest], a_recv.at[a, me], (view, dest))
-
     def mate(r, n):
         other = r + 1 - 2 * lax.rem(r, 2) if n % 2 else r
         return lax.rem(other + 2, group) if n >= 2 else other
+
+    next_dev = (view, lax.rem(me + 1, toks))
 
     def a2a_send(a, columns=GX):
         for gx in columns:
             for n in range(4):
                 if (gx, n) != (0, 0):
-                    a2a_copy(a, lax.rem(my_x + gx, XS) * group + mate(my_r, n)).start()
-
-    def a2a_wait(a, gx, mates=range(4)):
-        for n in mates:
-            if (gx, n) != (0, 0):
-                src = lax.rem(my_x + XS - gx, XS) * group + mate(my_r, n)
-                remote(stages[a].at[0], bufs[a].at[src], a_send.at[a, 0], a_recv.at[a, src], (view, src)).wait_recv()
+                    dest = lax.rem(my_x + gx, XS) * group + mate(my_r, n)
+                    sem = 5 + a if a else n - 1 if gx == 0 else 2 + GX.index(gx)
+                    remote(
+                        stages[a].at[unit_of(dest)], bufs[a].at[me], a_send.at[a], a_recv.at[sem], (view, dest)
+                    ).start()
+
+    def a2a_all(a):
+        part = pl.ds(0, 15)
+        return remote(stages[a].at[part], bufs[a].at[part], a_send.at[a], a_recv.at[5 + a], next_dev)
+
+    def a2a_wait_tile(n):
+        src = my_x * group + mate(my_r, n)
+        remote(stage_k.at[0], kbuf.at[src], a_send.at[0], a_recv.at[n - 1], next_dev).wait_recv()
+
+    def a2a_wait_column(gi):
+        part = pl.ds(lax.rem(my_x + XS - GX[gi], XS) * group, 4)
+        remote(stage_k.at[pl.ds(0, 4)], kbuf.at[part], a_send.at[0], a_recv.at[2 + gi], next_dev).wait_recv()
+
+    def z_recv_sem(a, hop, part):
+        if hop >= 2:
+            return z_recv.at[30 + a * 2 + hop - 2]
+        return z_recv.at[(14 + (a - 1) * 8 + hop * 4 if a else hop * 7) + part]
 
     def z_copy(a, hop, gi, gx):
         start = lax.rem(my_x + XS - gx, XS) * group
@@ -132,7 +146,13 @@
                 src = buf.at[pl.ds((src_set - 1) * toks + start, 4)]
             dst = buf.at[pl.ds((dst_set - 1) * toks + start, 4)]
         sem = gi + 3 if a == 0 else gi
-        return remote(src, dst, z_send.at[a, hop, sem], z_recv.at[a, hop, sem], dev)
+        return remote(src, dst, z_send.at[a, hop], z_recv_sem(a, hop, sem), dev)
+
+    def z_all(a, hop):
+        dst_set, dev = ((1, right_dev), (2, left_dev), (3, right_dev), (4, left_dev))[hop]
+        buf, lead = ((kbuf, 0), (vlow, 1), (vhigh, 1))[a]
+        part = buf.at[pl.ds((dst_set - lead) * toks, 16)]
+        return remote(part, part, z_send.at[a, hop], z_recv_sem(a, hop, 0), dev)
 
     def unit_place(by):
         return lax.rem(flip(me, lax.rem(upper + lax.rem(view + views + by, views) // half, 2)), group)
@@ -142,7 +162,7 @@
         src_set, dst_set, dev = ((0, 1, right_dev), (0, 2, left_dev), (1, 3, right_dev), (2, 4, left_dev))[hop]
         return remote(
             kbuf.at[src_set * toks + tile], kbuf.at[dst_set * toks + tile],
-            z_send.at[0, hop, n], z_recv.at[0, hop, n], dev,
+            z_send.at[0, hop], z_recv_sem(0, hop, n), dev,
         )
 
     def send_tile(n):
@@ -164,13 +184,8 @@
             z_copy(a, hop + 2, gi, gx).start()
 
     def wait_far(a):
-        if a == 0:
-            for n in range(4):
-                for hop, origin in ((2, -2), (3, 2)):
-                    z_tile(hop, n, origin).wait_recv()
-        for gi in range(1 if a == 0 else 0, 4):
-            for hop in (2, 3):
-                z_copy(a, hop, gi, GX[gi]).wait_recv()
+        for hop in (2, 3):
+            z_all(a, hop).wait_recv()
 
     stage_array(0)
     pl.semaphore_wait(barrier, 17)
@@ -178,24 +193,24 @@
     a2a_send(0, (0,))
     a2a_send(0, (1, 3))
     for n in range(1, 4):
-        a2a_wait(0, 0, (n,))
+        a2a_wait_tile(n)
         send_tile(n)
     a2a_send(0, (2,))
     stage_array(1)
     for gi in (1, 2):
-        a2a_wait(0, GX[gi])
+        a2a_wait_column(gi)
         send_own(0, gi, GX[gi])
     stage_array(2)
     a2a_send(1)
     a2a_send(2)
-    a2a_wait(0, GX[3])
+    a2a_wait_column(3)
     send_own(0, 3, GX[3])
     for n in range(4):
         send_tile_on(n)
     for gi in range(1, 4):
         send_on(0, gi, GX[gi])
+    a2a_all(1).wait_recv()
     for gi in range(4):
-        a2a_wait(1, GX[gi])
         send_own(1, gi, GX[gi])
 
     for table in tables[1:]:
@@ -216,8 +231,7 @@
             return carry
         lax.fori_loop(0, 16, count_row, 0)
 
-    for gx in GX:
-        a2a_wait(2, gx)
+    a2a_all(2).wait_recv()
     wait_far(0)
 
     sets = []
@@ -299,7 +313,11 @@
     lax.fori_loop(0, 16, weigh_step, 0)
 
     def o_copy(h, t):
-        return remote(obuf.at[h, t], orecv.at[h, unit_of(me)], o_send.at[h, t], o_recv.at[h, me], (view, t))
+        return remote(obuf.at[h, t], orecv.at[h, unit_of(me)], o_send.at[h], o_recv.at[h], (view, t))
+
+    def o_all(h):
+        part = pl.ds(0, 15)
+        return remote(obuf.at[h, part], orecv.at[h, part], o_send.at[h], o_recv.at[h], next_dev)
 
     for h in range(2):
         wait_far(1 + h)
@@ -331,9 +349,7 @@
         orecv[h, unit_of(me)] = obuf[h, me]
 
     for h in range(2):
-        for d in range(1, 16):
-            src = lax.rem(me + toks - d, toks)
-            remote(obuf.at[0, 0], orecv.at[h, unit_of(src)], o_send.at[h, 0], o_recv.at[h, src], (view, src)).wait_recv()
+        o_all(h).wait_recv()
     for s in range(2):
         role = first_slot if s == 0 else 1 - first_slot
         for p in range(8):
@@ -341,19 +357,12 @@
             out_ref[0, s, :HD, p * LANES:(p + 1) * LANES] = upper_rows
             out_ref[0, s, HD:, p * LANES:(p + 1) * LANES] = lower_rows
 
-    for d in range(1, 16):
-        peer = lax.rem(me + d, toks)
-        for a in range(3):
-            a2a_copy(a, peer).wait_send()
-        for h in range(2):
-            o_copy(h, peer).wait_send()
-    for n in range(4):
-        for hop, origin in ((0, 0), (1, 0), (2, -1), (3, 1)):
-            z_tile(hop, n, origin).wait_send()
     for a in range(3):
+        a2a_all(a).wait_send()
         for hop in range(4):
-            for gi in range(1 if a == 0 else 0, 4):
-                z_copy(a, hop, gi, GX[gi]).wait_send()
+            z_all(a, hop).wait_send()
+    for h in range(2):
+        o_all(h).wait_send()
 
 
 def local(queries, keys, values, tile_mask, offsets, branch_slots):
@@ -388,12 +397,12 @@
             pltpu.SMEM((NB, 16), jnp.int32),
             pltpu.SMEM((NB, 16), jnp.int32),
             dma((6,)),
-            dma((3, 16)),
-            dma((3, 16)),
-            dma((3, 4, 7)),
-            dma((3, 4, 7)),
-            dma((2, 16)),
-            dma((2, 16)),
+            dma((3,)),
+            dma((8,)),
+            dma((3, 4)),
+            dma((36,)),
+            dma((2,)),
+            dma((2,)),
         ],
         compiler_params=pltpu.CompilerParams(
             collective_id=0, has_side_effects=True, vmem_limit_bytes=VMEM_BYTES

time: 77.9 us -> 75.3 us (0.967)
  Pallas kernels: 75.8 us -> 73.2 us
    pallas_call x1, Pallas kernels: 75.8 us -> 73.2 us  [local(): pl.pallas_call(attend_kernel, out_shape=jax.ShapeDtypeStruct(queries.shap...]
where the time goes in v5:
time: 75.3 us; the launch traced here: 75.1 us
  Pallas kernels  73.2 us (97%)
  local copies, waits for them, and re-layouts  1.87 us (2%)
    pallas_call x1, Pallas kernels, local(): pl.pallas_call(attend_kernel, out_shape=jax.ShapeDtypeStruct(queries.shap...  73.2 us
    unnamed x1, local copies, waits for them, and re-layouts  1.87 us

profile of v5, /device:TPU:1, one launch (start us, length us, event | category | flops | bytes accessed | tf_op | source)
XLA Modules:
  0.0 75.1 jit_solution(3348644728892182230)
XLA Ops:
  0.0 73.2 %shard_map.64 = bf16[1,2,128,1024]{3,2,1,0:T(8,128)(2,1)} custom-call(s32[1,2,16,16]{3,2,1,0:T(8,128)} %mask_in.1, s32[1,2]{1,0:T(1,128)} %off_in.1, s32[2,32]{1,0:T(2,128)} %bitcast.1, bf16[1,2,128,1024]{3,2,1,0:T(8,128)(2,1)} %q_ref.1, bf16[1,2,128,1024]{3,2,1,0:T(8,128)(2,1)} %k_ref.1, bf16[1,2,128,1024]{3,2,1,0:T(8,128)(2,1)} %v_ref.1), custom_call_target="tpu_custom_call" | custom-call | flops 3500000000 | bytes 2097152 | tf_op jit(solution)/shard_map/pallas_call | solution.py:372
  73.3 1.9 %copy.8 = bf16[1,2,128,1024]{3,2,1,0:T(8,128)(2,1)} copy(bf16[1,2,128,1024]{3,2,1,0:T(8,128)(2,1)} %shard_map.64) | data formatting | bytes 1048576
